TPU v7x, 512 devices: a whole 4x4x16 slice. The times are simulated.
512 devices in a mesh: member: 8 (over z_hi, y), band: 64 (over x, z_lo, core).
Axes of the slice: x: 4, y: 4, z: 16 (z_hi: 2, z_lo: 8; z = z_hi * 8 + z_lo), core: 2. Of those that a mesh axis runs over, the one named last changes fastest.
Arguments:
- mesh_latent: bfloat16 [8, 8192, 512], P('member', 'band'), may hold values from -6 to 6
- grid_latent: bfloat16 [8, 20480, 512], P('member', 'band'), may hold values from -16 to 16
- senders: int32 [20480, 3], P('band'), may hold values from 0 to 191, as said below
- live_points: int32 [64], replicated, may hold values from 80 to 320, as said below
- target: bfloat16 [100, 20480], P(None, 'band'), may hold values from -6 to 6
- w_send: bfloat16 [512, 512], replicated, may hold values from -0.25 to 0.25
- w_recv: bfloat16 [512, 512], replicated, may hold values from -0.25 to 0.25
- w_edge: bfloat16 [512, 512], replicated, may hold values from -0.25 to 0.25
- w_out: bfloat16 [512, 100], replicated, may hold values from -0.25 to 0.25
- gain: float32 [512], replicated, may hold values from 0.5 to 1.5
Outputs:
- crps_field: float32 [20480], P('band')
- grad_send: float32 [512, 512], P('band')
- grad_recv: float32 [512, 512], P('band')
- grad_edge: float32 [512, 512], P('band')
- grad_out: float32 [512, 100], P('band')
Inputs may be any that keep to these rules, and one draw needn't show every extreme that they name: `senders`: index into the band's 128 own mesh rows extended by 32 rows of each neighbouring band (index 32 is the band's first own row; rows beyond the poles are zero). `live_points`: positions at or past a band's count are padding.
All inputs are finite; a program needn't handle non-finite values.
Results may differ from a plain program's by a relative error of at most 0.012.
Values may be sent and summed in bfloat16 or wider, within the bound.
A program may use at most 64 MiB of HBM per device.

v0:
```python
import jax
import jax.numpy as jnp
from jax import lax
from jax.sharding import PartitionSpec as P

HALO = 32


smooth_sq = 0.0625


def extended(block, sides, width):
    for axis, dim in sides:
        count = lax.axis_size(axis)
        forward = [(i, i + 1) for i in range(count - 1)]
        backward = [(target, source) for source, target in forward]
        low = lax.ppermute(
            lax.slice_in_dim(block, block.shape[dim] - width, None, axis=dim), axis, forward
        )
        high = lax.ppermute(lax.slice_in_dim(block, 0, width, axis=dim), axis, backward)
        block = jnp.concatenate([low, block, high], axis=dim)
    return block


def decode_band(grid_rows, mesh_rows, sender_rows, w_send, w_recv, w_edge, w_out, gain):
    sent_rows = jnp.dot(mesh_rows, w_send, preferred_element_type=jnp.float32)
    recv_rows = jnp.dot(grid_rows, w_recv, preferred_element_type=jnp.float32)
    preact = jnp.take(sent_rows, sender_rows, axis=0) + recv_rows[:, None, :]
    agg_in = jnp.sum(jax.nn.silu(preact), axis=1).astype(jnp.bfloat16)
    hidden_sum = grid_rows.astype(jnp.float32) + jnp.dot(
        agg_in, w_edge, preferred_element_type=jnp.float32
    )
    inv_rms = lax.rsqrt(jnp.mean(hidden_sum * hidden_sum, axis=1, keepdims=True) + 1e-05)
    normed = (hidden_sum * inv_rms * gain).astype(jnp.bfloat16)
    pred = lax.dot_general(
        w_out, normed, (((0,), (1,)), ((), ())), preferred_element_type=jnp.float32
    )
    return (pred.astype(jnp.bfloat16), (preact, agg_in, hidden_sum, inv_rms, normed))


def backward_band(field_grad, grid_rows, mesh_rows, sender_rows, saved, w_edge, w_out, gain):
    preact, agg_in, hidden_sum, inv_rms, normed = saved
    grad16 = field_grad.astype(jnp.bfloat16)
    d_out = lax.dot_general(
        normed, grad16, (((0,), (1,)), ((), ())), preferred_element_type=jnp.float32
    )
    d_normed = lax.dot_general(
        grad16, w_out, (((0,), (1,)), ((), ())), preferred_element_type=jnp.float32
    )
    gained = d_normed * gain
    d_hidden = inv_rms * gained - hidden_sum * inv_rms**3 * jnp.mean(
        gained * hidden_sum, axis=1, keepdims=True
    )
    d_hidden = d_hidden.astype(jnp.bfloat16)
    d_edge = lax.dot_general(
        agg_in, d_hidden, (((0,), (0,)), ((), ())), preferred_element_type=jnp.float32
    )
    d_aggin = lax.dot_general(
        d_hidden, w_edge, (((1,), (1,)), ((), ())), preferred_element_type=jnp.float32
    )
    sigmoid_v = jax.nn.sigmoid(preact)
    d_preact = d_aggin[:, None, :] * sigmoid_v * (1.0 + preact * (1.0 - sigmoid_v))
    d_recv = jnp.sum(d_preact, axis=1).astype(jnp.bfloat16)
    d_recvw = lax.dot_general(
        grid_rows, d_recv, (((0,), (0,)), ((), ())), preferred_element_type=jnp.float32
    )
    width = d_preact.shape[2]
    d_sent = jax.ops.segment_sum(
        d_preact.reshape(-1, width), sender_rows.reshape(-1), num_segments=mesh_rows.shape[0]
    )
    d_sent = d_sent.astype(jnp.bfloat16)
    d_sendw = lax.dot_general(
        mesh_rows, d_sent, (((0,), (0,)), ((), ())), preferred_element_type=jnp.float32
    )
    return (d_sendw, d_recvw, d_edge, d_out)


def pair_terms(fields, target, live_mask, scale):
    count = fields.shape[0]
    values = fields.astype(jnp.float32)
    truth = target.astype(jnp.float32)
    error = values - truth
    root_error = jnp.sqrt(error * error + smooth_sq)
    abs_error = jnp.sum(root_error, axis=0) / count
    spread = jnp.zeros(truth.shape, jnp.float32)
    pair_slope = jnp.zeros(values.shape, jnp.float32)
    for other in range(count):
        differ = values - values[other]
        root_differ = jnp.sqrt(differ * differ + smooth_sq)
        spread = spread + jnp.sum(root_differ, axis=0)
        pair_slope = pair_slope + differ / root_differ
    crps = jnp.sum(abs_error - spread / (2.0 * count * (count - 1)), axis=0) * live_mask
    field_grad = (error / root_error / count - pair_slope / (count * (count - 1))) * (
        live_mask * scale
    )
    return (crps, field_grad)


def per_device(
    mesh_latent, grid_latent, senders, live_points, target, w_send, w_recv, w_edge, w_out, gain
):
    mesh_rows = extended(mesh_latent[0], (("band", 0),), HALO)
    grid_rows = grid_latent[0]
    pred, saved = decode_band(grid_rows, mesh_rows, senders, w_send, w_recv, w_edge, w_out, gain)
    band_index = lax.axis_index("band")
    member_index = lax.axis_index("member")
    slots = grid_rows.shape[0]
    live_count = live_points[band_index]
    live_mask = (jnp.arange(slots, dtype=jnp.int32) < live_count).astype(jnp.float32)
    scale = 1.0 / (jnp.sum(live_points).astype(jnp.float32) * target.shape[0])
    fields = lax.all_gather(pred[None], "member", axis=0, tiled=True)
    crps_field, all_grads = pair_terms(fields, target, live_mask, scale)
    field_grad = lax.dynamic_index_in_dim(all_grads, member_index, 0, keepdims=False)
    gradients = backward_band(field_grad, grid_rows, mesh_rows, senders, saved, w_edge, w_out, gain)
    summed = (
        lax.psum(gradients[0].astype(jnp.bfloat16), "member").astype(jnp.float32),
        lax.psum(gradients[1].astype(jnp.bfloat16), "member").astype(jnp.float32),
        lax.psum(gradients[2].astype(jnp.bfloat16), "member").astype(jnp.float32),
        lax.psum(gradients[3].astype(jnp.bfloat16), "member").astype(jnp.float32),
    )
    result = (
        lax.psum_scatter(summed[0], "band", scatter_dimension=0, tiled=True),
        lax.psum_scatter(summed[1], "band", scatter_dimension=0, tiled=True),
        lax.psum_scatter(summed[2], "band", scatter_dimension=0, tiled=True),
        lax.psum_scatter(summed[3], "band", scatter_dimension=0, tiled=True),
    )
    return (crps_field, result[0], result[1], result[2], result[3])


def solution(mesh):
    placed = (
        P("member", "band", None),
        P("member", "band", None),
        P("band", None),
        P(),
        P(None, "band"),
        P(),
        P(),
        P(),
        P(),
        P(),
    )
    return jax.shard_map(
        per_device,
        mesh=mesh,
        in_specs=placed,
        out_specs=(P("band"), P("band", None), P("band", None), P("band", None), P("band", None)),
        check_vma=False,
    )
```

profile of v0, /device:TPU:8, one launch (start us, length us, event | category | flops | bytes accessed | tf_op | source)
XLA Modules:
  0.0 1675.5 jit_solution(2602064763403687491)
XLA Ops:
  7.2 1.4 slice_bitcast_fusion.9
  8.7 1.7 collective-permute-start
  10.4 1.3 collective-permute-start.1
  11.7 0.7 compare_select_fusion
  12.4 0.7 compare_and_fusion
  13.3 0.2 reshape.52
  13.5 1.3 reduce_sum.147
  14.8 1.2 dynamic_slice.7
  16.6 2.3 fusion.52
  19.0 0.5 fusion.69
  19.7 0.2 copy.27
  19.9 0.7 convert_element_type.73
  20.6 1.5 add.149
  22.1 2.0 add.179
  24.1 0.2 broadcast_in_dim.37
  24.3 0.8 reshape.60
  25.1 1.3 fusion.66
  26.4 4.8 gather_fusion
  31.3 2.8 reshape.51
  34.1 4.2 multiply_reduce_fusion.1
  38.3 0.4 multiply_reduce_fusion.3
  38.8 0.4 copy-done.18
  39.2 0.3 fusion.47
  39.5 75.9 %all-gather.1 = bf16[8,100,320]{2,1,0:T(8,128)(2,1)S(1)} all-gather(bf16[1,100,320]{2,1,0:T(8,128)(2,1)S(1)} %fusion.47), channel_id=2, replica_groups=mesh['member'=8,'band'=64] {'member'}, dimensions={0}, use_global_device_ids=true | all-gather | bytes 576000 | tf_op jit(solution)/shard_map/all_gather | solution.py:111
  115.7 0.8 copy-done.6
  116.5 7.0 fusion.73
  123.6 0.4 multiply_reduce_fusion.2
  124.0 0.2 subtract_convert_fusion
  124.2 0.4 fusion.76
  124.6 1.3 convolution_convert_fusion
  125.9 1.0 convolution_convert_fusion.3
  126.9 4.6 multiply_reduce_fusion
  131.5 2.0 mul.154
  133.4 4.4 mul.155
  137.8 1.3 fusion.46
  139.1 9.7 scatter_custom_fusion
  148.7 1.9 convolution_convert_fusion.2
  150.7 212.9 %all-reduce.5.cloned.1.call-done = (bf16[512,512]{0,1:T(8,128)(2,1)}, bf16[512,100]{1,0:T(8,128)(2,1)}, bf16[512,512]{1,0:T(8,128)(2,1)}, bf16[512,512]{1,0:T(8,128)(2,1)}) async-done(((bf16[512,512]{0,1:T(8,128)(2,1)}, bf16[512,100]{1,0:T(8,128)(2,1)}, bf16[512,512]{1,0:T(8,128)(2,1)}, bf16[512,512]{1,0:T(8,128)(2,1)}), (bf16[512,512]{0,1:T(8,128)(2,1)}, bf16[512,100]{1,0:T(8,128)(2,1)}, ...) | async-done | bytes 1675280 | tf_op jit(solution)/shard_map/psum | solution.py:117
  363.6 2.3 copy.32
  366.0 1.2 convert_element_type.80
  367.4 1.1 convert_element_type.86
  368.5 1.3 dynamic-slice
  370.7 1.1 fusion.70
  371.8 419.1 %all-reduce.6 = f32[512,100]{1,0:T(8,128)S(1)} all-reduce(bf16[512,100]{1,0:T(8,128)(2,1)S(1)} %copy-done.20), channel_id=6, replica_groups=mesh['member'=8,'band'=64] {'band'}, use_global_device_ids=true, to_apply=%region_23.24.clone | all-reduce | flops 51200 | bytes 307200
  791.0 0.6 constant_dynamic-slice_fusion
  791.6 13.2 reduce-scatter.10.cloned.1.call-done
  804.8 431.8 %reduce-scatter.6.cloned.1.call-done = f32[8,512]{1,0:T(8,128)} async-done(((f32[512,512]{1,0:T(8,128)}), f32[8,512]{1,0:T(8,128)}) %reduce-scatter.6.cloned.1.call-update) | async-done | bytes 16400 | tf_op jit(solution)/shard_map/reduce_scatter | solution.py:122
  1236.6 432.4 %reduce-scatter.8.cloned.1.call-done = f32[8,512]{1,0:T(8,128)} async-done(((f32[512,512]{1,0:T(8,128)}), f32[8,512]{1,0:T(8,128)}) %reduce-scatter.8.cloned.1.call-update) | async-done | bytes 16400 | tf_op jit(solution)/shard_map/reduce_scatter | solution.py:124
  (65 shorter events, 1.0 us)
Async XLA Ops:
  7.2 31.1 %copy-start = (bf16[512,512]{1,0:T(8,128)(2,1)S(1)}, bf16[512,512]{1,0:T(8,128)(2,1)}, u32[]{:S(2)}) copy-start(bf16[512,512]{1,0:T(8,128)(2,1)} %param.17) | copy-start | bytes 1572868
  7.2 12.4 copy-start.22
  7.2 12.7 copy-start.21
  7.2 356.4 %all-reduce.5.cloned.1.call-start = ((), (), s32[]{:S(2)}) async-start(), calls=%async_computation.6 | async-start | bytes 3407872 | tf_op jit(solution)/shard_map/psum | solution.py:117
  8.7 16.4 collective-permute-start
  10.4 14.7 collective-permute-start.1
  22.1 3.0 copy-start.4
  34.1 4.2 copy-start.3
  38.3 0.9 copy-start.18
  38.3 0.9 copy-start.23
  115.6 0.9 copy-start.6
  124.6 2.3 copy-start.2
  133.4 4.4 copy-start.19
  133.4 5.6 copy-start.1
  139.1 9.7 copy-start.5
  150.7 654.1 %reduce-scatter.10.cloned.1.call-start = ((), (), s32[]{:S(2)}) async-start(), calls=%async_computation.5 | async-start | bytes 1064960
  363.6 2.4 copy-start.17
  366.0 870.6 %reduce-scatter.6.cloned.1.call-start = ((), (), s32[]{:S(2)}) async-start(), calls=%async_computation.3 | async-start | bytes 1064960 | tf_op jit(solution)/shard_map/reduce_scatter | solution.py:122
  366.0 1.3 copy-start.16
  367.2 1301.7 %reduce-scatter.8.cloned.1.call-start = ((), (), s32[]{:S(2)}) async-start(), calls=%async_computation.4 | async-start | bytes 1064960 | tf_op jit(solution)/shard_map/reduce_scatter | solution.py:124
  367.3 3.2 copy-start.7
  367.3 3.2 copy-start.8
  367.3 3.2 copy-start.9
  367.3 3.2 copy-start.10
  367.3 3.2 copy-start.11
  367.3 3.2 copy-start.12
  367.4 3.2 copy-start.13
  367.4 3.2 copy-start.14
  367.4 3.2 copy-start.15
  368.5 3.3 copy-start.20
Sparse Core Ops, SparseCore 0:
  150.8 212.7 all-reduce.4
  367.2 437.5 reduce-scatter.9
  808.2 428.3 reduce-scatter.5
  1240.0 428.8 reduce-scatter.7
where the time goes:
time: 1680 us
  waiting for transfers between devices  1090 us (65%)
  blocking collectives  495 us (29%)
  other arithmetic  33.2 us (2%)
  local copies, waits for them, and re-layouts  27.4 us (2%)
    reduce_scatter x1, waiting for transfers between devices, per_device(): lax.psum_scatter(summed[2], 'band', scatter_dimension=0, tiled=True)  432 us
    reduce_scatter x1, waiting for transfers between devices, per_device(): lax.psum_scatter(summed[0], 'band', scatter_dimension=0, tiled=True)  432 us
    unnamed x1, blocking collectives  419 us
    psum x1, waiting for transfers between devices, per_device(): lax.psum(gradients[1].astype(jnp.bfloat16), 'member').astype(jnp.float32)  213 us
    all_gather x1, blocking collectives, per_device(): fields = lax.all_gather(pred[None], 'member', axis=0, tiled=True)  75.9 us
  transfers between devices with their start and end apart: 6, of which 4 were waited for; matrix products, arithmetic and copies ran while one was open for 1% of the time, Pallas kernels for 0%

commit v1 on v0

v1 whole, which is shorter than its diff:
```python
import jax
import jax.numpy as jnp
from jax import lax
from jax.experimental import pallas as pl
from jax.experimental.pallas import tpu as pltpu
from jax.sharding import PartitionSpec as P

HALO = 32
SMOOTH_SQ = 0.0625
MESH = pl.DeviceIdType.MESH
F32 = jnp.float32
BF16 = jnp.bfloat16

D = 512
VARS = 100
PTS = 320
OWN = 128
ROWS = OWN + 2 * HALO
PACK = 256
TAIL = PTS - PACK
FOLD = 25


def dot(a, b, dims=((1,), (0,))):
    return lax.dot_general(a, b, (dims, ((), ())), preferred_element_type=F32)


def lanes_of(shape):
    return lax.broadcasted_iota(jnp.int32, shape, 1)


def rows_of(shape):
    return lax.broadcasted_iota(jnp.int32, shape, 0)


def pack_field(x):
    tail = x[PACK:]
    lane = lanes_of(tail.shape)
    inside = (lane >= VARS) & (lane < VARS + FOLD)
    parts = [jnp.where(inside, pltpu.roll(tail, VARS - FOLD * j, 1), 0.0) for j in range(4)]
    return x[:PACK] + jnp.concatenate(parts, axis=0)


def unpack_field(x):
    lane = lanes_of((TAIL, 128))
    tail = jnp.zeros((TAIL, 128), F32)
    for j in range(4):
        moved = pltpu.roll(x[TAIL * j : TAIL * (j + 1)], 128 - (VARS - FOLD * j), 1)
        tail = tail + jnp.where((lane >= FOLD * j) & (lane < FOLD * (j + 1)), moved, 0.0)
    main = jnp.where(lanes_of((PACK, 128)) < VARS, x, 0.0)
    return jnp.concatenate([main, tail], axis=0)


def kernel(
    mesh_ref, grid_ref, send_ref, live_ref, target_ref, ws_ref, wr_ref, we_ref, wo_ref, gain_ref,
    crps_out, gs_out, gr_out, ge_out, go_out,
    halo, wo, tpad, spad, onehot_t, slope_k, fields, crow, crow_z,
    part, core_in, summed, x_in1, x_sum1, y_in1, y_in2, y_sum2, x_in2, slab, z_in, final,
    s_halo, r_halo, s_fz, r_fz, s_fy, r_fy, s_fzy, r_fzy, s_cy, r_cy, s_cz, r_cz,
    s_core, r_core, s_x1, r_x1, s_y1, r_y1, s_y2, r_y2, s_x2, r_x2, s_z, r_z, s_g, r_g,
):
    member = lax.axis_index("member")
    band = lax.axis_index("band")
    zh, y = member // 4, member % 4
    x, zl, c = band // 16, (band // 2) % 8, band % 2
    z = zh * 8 + zl

    def dev(z_, y_, x_, c_):
        return ((z_ // 8) * 4 + y_, x_ * 16 + (z_ % 8) * 2 + c_)

    def z_peer(k):
        return dev((z + k) % 16, y, x, c)

    def y_peer(k):
        return dev(z, (y + k) % 4, x, c)

    def x_peer(k):
        return dev(z, y, (x + k) % 4, c)

    sibling = dev(z, y, x, 1 - c)
    upper = (member, (band + 1) % 64)
    lower = (member, (band + 63) % 64)
    other = (member, (band + 2 * c - 1 + 64) % 64)

    def rcopy(src, dst, ss, rs, to):
        return pltpu.make_async_remote_copy(
            src_ref=src, dst_ref=dst, send_sem=ss, recv_sem=rs, device_id=to, device_id_type=MESH
        )

    barrier = pltpu.get_barrier_semaphore()
    peers = [z_peer(k) for k in range(1, 16)]
    peers += [y_peer(k) for k in (1, 2, 3)] + [x_peer(k) for k in (1, 2, 3)]
    peers += [sibling, other]
    for p in peers:
        pl.semaphore_signal(barrier, inc=1, device_id=p, device_id_type=MESH)

    sent_own = dot(mesh_ref[...], ws_ref[...])
    recv_rows = dot(grid_ref[...], wr_ref[...])
    wo[...] = jnp.zeros(wo.shape, BF16)
    wo[:, :VARS] = wo_ref[...]
    tpad[...] = jnp.zeros(tpad.shape, F32)
    tpad[:VARS, :PTS] = target_ref[...].astype(F32)
    truth = pack_field(jnp.transpose(tpad[...])[:PTS])
    spad[...] = jnp.zeros(spad.shape, F32)
    spad[:PTS, :3] = send_ref[...].astype(F32)
    senders_t = jnp.transpose(spad[...])[:8, :PTS].astype(jnp.int32)

    def moved(s):
        return jnp.where(s < HALO, s + OWN, jnp.where(s < HALO + OWN, s - HALO, s))

    index = moved(send_ref[...])
    index_t = moved(senders_t)
    for k in range(3):
        hit = rows_of((ROWS, PTS)) == index_t[k : k + 1, :]
        onehot_t[k] = jnp.where(hit, 1.0, 0.0).astype(BF16)
    live = live_ref[...]
    lane64 = lanes_of(live.shape)
    count = jnp.sum(jnp.where(lane64 == band, live, 0).astype(F32), axis=1, keepdims=True)
    total = jnp.sum(live.astype(F32), axis=1, keepdims=True)
    scale = 1.0 / (total * VARS)
    row = rows_of((PACK, 128))
    lane = lanes_of((PACK, 128))
    point = jnp.where(lane < VARS, row, PACK + row % TAIL)
    mask = jnp.where((lane < VARS + FOLD) & (point.astype(F32) < count), 1.0, 0.0)

    pl.semaphore_wait(barrier, len(peers))

    halo_copies = []
    for i in range(2):
        for j in range(4):
            cols = pl.ds(128 * j, 128)
            up_src = mesh_ref.at[pl.ds(OWN - HALO + 16 * i, 16), cols]
            low_src = mesh_ref.at[pl.ds(16 * i, 16), cols]
            n = i * 4 + j
            halo_copies.append(
                rcopy(up_src, halo.at[0, pl.ds(16 * i, 16), cols], s_halo.at[0, n], r_halo.at[0, n], upper)
            )
            halo_copies.append(
                rcopy(low_src, halo.at[1, pl.ds(16 * i, 16), cols], s_halo.at[1, n], r_halo.at[1, n], lower)
            )
    for cp in halo_copies:
        cp.start()
    for cp in halo_copies:
        cp.wait()
    low = jnp.where(band == 0, 0.0, halo[0].astype(F32)).astype(BF16)
    high = jnp.where(band == 63, 0.0, halo[1].astype(F32)).astype(BF16)
    edge_rows = jnp.concatenate([low, high], axis=0)
    sent_edge = dot(edge_rows, ws_ref[...])
    sent = jnp.concatenate([sent_own, sent_edge], axis=0).astype(BF16)

    agg = jnp.zeros((PTS, D), F32)
    for k in range(3):
        hit = lanes_of((PTS, ROWS)) == index[:, k : k + 1]
        pre = dot(jnp.where(hit, 1.0, 0.0).astype(BF16), sent) + recv_rows
        sig = 0.5 * jnp.tanh(0.5 * pre) + 0.5
        act = pre * sig
        agg = agg + act
        slope_k[k] = sig + act * (1.0 - sig)
    agg_in = agg.astype(BF16)
    hidden = grid_ref[...].astype(F32) + dot(agg_in, we_ref[...])
    inv_rms = lax.rsqrt(jnp.mean(hidden * hidden, axis=1, keepdims=True) + 1e-05)
    gain = gain_ref[...]
    normed = (hidden * inv_rms * gain).astype(BF16)
    pred = dot(normed, wo[...])
    fields[0, 0] = pack_field(pred).astype(BF16)

    def rows(n):
        return pl.ds(64 * n, 64)

    fz = [
        rcopy(fields.at[0, 0, rows(n)], fields.at[1, 0, rows(n)], s_fz.at[n], r_fz.at[n], z_peer(8))
        for n in range(4)
    ]
    fy = [
        rcopy(fields.at[0, 0], fields.at[0, k], s_fy.at[k - 1], r_fy.at[k - 1], y_peer(k))
        for k in (1, 2, 3)
    ]
    fzy = [
        [
            rcopy(
                fields.at[1, 0, rows(n)], fields.at[1, k, rows(n)], s_fzy.at[k - 1, n], r_fzy.at[k - 1, n], y_peer(k)
            )
            for k in (1, 2, 3)
        ]
        for n in range(4)
    ]
    for cp in fz + fy:
        cp.start()

    own = fields[0, 0].astype(F32)
    error = own - truth
    error_sq = error * error + SMOOTH_SQ
    error_inv = lax.rsqrt(error_sq)
    pair_slope = jnp.zeros((PACK, 128), F32)
    spread = jnp.full((PACK, 128), 0.25, F32)

    def pair(h, k, pair_slope, spread):
        differ = own - fields[h, k].astype(F32)
        sq = differ * differ + SMOOTH_SQ
        inv = lax.rsqrt(sq)
        return pair_slope + differ * inv, spread + sq * inv

    for k in (1, 2, 3):
        fy[k - 1].wait_recv()
        pair_slope, spread = pair(0, k, pair_slope, spread)
    for n in range(4):
        fz[n].wait_recv()
        for cp in fzy[n]:
            cp.start()
    pair_slope, spread = pair(1, 0, pair_slope, spread)
    for k in (1, 2, 3):
        for n in range(4):
            fzy[n][k - 1].wait_recv()
        pair_slope, spread = pair(1, k, pair_slope, spread)

    field_grad = (error * error_inv * 0.125 - pair_slope * (1.0 / 56.0)) * (mask * scale)
    grad16 = unpack_field(field_grad).astype(BF16)

    crps = (error_sq * error_inv * 0.125 - spread * (1.0 / 112.0)) * mask
    crps_hi = crps.astype(BF16)
    crps_lo = (crps - crps_hi.astype(F32)).astype(BF16)
    lane8 = lanes_of((8, 128))
    take_main = jnp.where(lane8 < VARS, 1.0, 0.0).astype(BF16)
    take_tail = jnp.where((lane8 >= VARS) & (lane8 < VARS + FOLD), 1.0, 0.0).astype(BF16)
    across = ((1,), (1,))
    main = dot(take_main, crps_hi, across) + dot(take_main, crps_lo, across)
    tail = dot(take_tail, crps_hi, across) + dot(take_tail, crps_lo, across)
    tail = tail[:, :128] + tail[:, 128:]
    tail = tail + pltpu.roll(tail, 64, 1)
    crow[0, :, :256] = main
    crow[0, :, 256:] = tail
    cy = [rcopy(crow.at[0], crow.at[k], s_cy.at[k - 1], r_cy.at[k - 1], y_peer(k)) for k in (1, 2, 3)]
    for cp in cy:
        cp.start()

    def store_part(q, full):
        if q == 3:
            wide = full.reshape(64, 8, 128)
            block = jnp.concatenate([wide, jnp.zeros_like(wide)], axis=1).astype(BF16)
            block = block.reshape(4, 8, 2, 16, 128)
            for cc in range(2):
                part[cc, q, :, :, :, :128] = block[:, :, cc]
                part[cc, q, :, :, :, 128:] = jnp.zeros((4, 8, 16, 128), BF16)
        else:
            left = full[:, :256].reshape(64, 8, 256)
            right = full[:, 256:].reshape(64, 8, 256)
            block = jnp.concatenate([left, right], axis=1).astype(BF16).reshape(4, 8, 2, 16, 256)
            for cc in range(2):
                part[cc, q] = block[:, :, cc]

    core = [rcopy(part.at[1 - c, q], core_in.at[q], s_core.at[q], r_core.at[q], sibling) for q in range(4)]
    depth = ((0,), (0,))
    d_normed = dot(grad16, wo[...], ((1,), (1,)))
    store_part(3, dot(normed, grad16, depth))
    core[3].start()
    gained = d_normed * gain
    mean = jnp.mean(gained * hidden, axis=1, keepdims=True)
    d_hidden = (inv_rms * gained - hidden * (inv_rms * inv_rms * inv_rms * mean)).astype(BF16)
    d_agg = dot(d_hidden, we_ref[...], ((1,), (1,)))
    store_part(2, dot(agg_in, d_hidden, depth))
    core[2].start()
    d_recv = jnp.zeros((PTS, D), F32)
    d_sent = jnp.zeros((ROWS, D), F32)
    for k in range(3):
        d_pre = d_agg * slope_k[k]
        d_recv = d_recv + d_pre
        d_sent = d_sent + dot(onehot_t[k], d_pre.astype(BF16))
    store_part(1, dot(grid_ref[...], d_recv.astype(BF16), depth))
    core[1].start()
    d_sent = d_sent.astype(BF16)
    store_part(0, dot(mesh_ref[...], d_sent[:OWN], depth) + dot(edge_rows, d_sent[OWN:], depth))
    core[0].start()

    x1 = [
        [
            rcopy(
                summed.at[q, (x + k) % 4, pl.ds(0, 4)], x_in1.at[q, k - 1], s_x1.at[q, k - 1], r_x1.at[q, k - 1], x_peer(k)
            )
            for k in (1, 2, 3)
        ]
        for q in range(4)
    ]
    for q in (3, 2, 1, 0):
        core[q].wait_recv()
        summed[q] = (part[c, q].astype(F32) + core_in[q].astype(F32)).astype(BF16)
        for cp in x1[q]:
            cp.start()
    y2 = [
        rcopy(summed.at[(y + k) % 4, :, pl.ds(4, 4)], y_in2.at[k - 1], s_y2.at[k - 1], r_y2.at[k - 1], y_peer(k))
        for k in (1, 2, 3)
    ]
    for cp in y2:
        cp.start()

    for cp in cy:
        cp.wait_recv()
    crow_z[0] = (crow[0] + crow[1]) + (crow[2] + crow[3])
    cz = rcopy(crow_z.at[0], crow_z.at[1], s_cz.at[0], r_cz.at[0], z_peer(8))
    cz.start()

    def add4(a, b0, b1, b2):
        return ((a.astype(F32) + b0.astype(F32)) + (b1.astype(F32) + b2.astype(F32))).astype(BF16)

    y1 = [
        rcopy(x_sum1.at[(y + k) % 4], y_in1.at[k - 1], s_y1.at[k - 1], r_y1.at[k - 1], y_peer(k))
        for k in (1, 2, 3)
    ]
    x2 = [
        rcopy(y_sum2.at[(x + k) % 4], x_in2.at[k - 1], s_x2.at[k - 1], r_x2.at[k - 1], x_peer(k))
        for k in (1, 2, 3)
    ]
    for q in (3, 2, 1, 0):
        for cp in x1[q]:
            cp.wait_recv()
        x_sum1[q] = add4(summed[q, x, 0:4], x_in1[q, 0], x_in1[q, 1], x_in1[q, 2])
    for cp in y1:
        cp.start()
    for cp in y2:
        cp.wait_recv()
    y_sum2[...] = add4(summed[y, :, 4:8], y_in2[0], y_in2[1], y_in2[2])
    for cp in x2:
        cp.start()
    for cp in y1:
        cp.wait_recv()
    slab[0:4] = add4(x_sum1[y], y_in1[0], y_in1[1], y_in1[2])
    for cp in x2:
        cp.wait_recv()
    slab[4:8] = add4(y_sum2[x], x_in2[0], x_in2[1], x_in2[2])

    zs = [
        rcopy(slab.at[(zl + k) % 8], z_in.at[k - 1], s_z.at[k - 1], r_z.at[k - 1], z_peer(k))
        for k in range(1, 16)
    ]
    order = (8, 7, 9, 6, 10, 5, 11, 4, 12, 3, 13, 2, 14, 1, 15)
    for k in order:
        zs[k - 1].start()
    acc = slab[zl].astype(F32)
    for k in reversed(order):
        zs[k - 1].wait_recv()
        acc = acc + z_in[k - 1].astype(F32)
    final[0] = acc
    gy = [rcopy(final.at[0], final.at[k], s_g.at[k - 1], r_g.at[k - 1], y_peer(k)) for k in (1, 2, 3)]
    for cp in gy:
        cp.start()
    cz.wait_recv()
    crps_out[...] = (crow_z[0] + crow_z[1])[:1, :PTS]
    for cp in gy:
        cp.wait_recv()

    def piece(q):
        return final[(y - q + 4) % 4]

    for q, out in ((0, gs_out), (1, gr_out), (2, ge_out)):
        got = piece(q)
        out[:, :256] = got[:8]
        out[:, 256:] = got[8:]
    go_out[...] = piece(3)[:8, :VARS]

    sends = fz + fy + [cp for g in fzy for cp in g] + cy + [cz] + core
    sends += [cp for g in x1 for cp in g] + y1 + y2 + x2 + zs + gy
    for cp in sends:
        cp.wait_send()


def per_device(mesh_latent, grid_latent, senders, live_points, target, w_send, w_recv, w_edge, w_out, gain):
    vmem = pl.BlockSpec(memory_space=pltpu.VMEM)
    dma = pltpu.SemaphoreType.DMA
    shape = jax.ShapeDtypeStruct
    outs = pl.pallas_call(
        kernel,
        out_shape=(
            shape((1, PTS), F32),
            shape((8, D), F32),
            shape((8, D), F32),
            shape((8, D), F32),
            shape((8, VARS), F32),
        ),
        in_specs=[vmem] * 10,
        out_specs=[vmem] * 5,
        scratch_shapes=[
            pltpu.VMEM((2, HALO, D), BF16),
            pltpu.VMEM((D, 128), BF16),
            pltpu.VMEM((128, 384), F32),
            pltpu.VMEM((384, 128), F32),
            pltpu.VMEM((3, ROWS, PTS), BF16),
            pltpu.VMEM((3, PTS, D), F32),
            pltpu.VMEM((2, 4, PACK, 128), BF16),
            pltpu.VMEM((4, 8, 384), F32),
            pltpu.VMEM((2, 8, 384), F32),
            pltpu.VMEM((2, 4, 4, 8, 16, 256), BF16),
            pltpu.VMEM((4, 4, 8, 16, 256), BF16),
            pltpu.VMEM((4, 4, 8, 16, 256), BF16),
            pltpu.VMEM((4, 3, 4, 16, 256), BF16),
            pltpu.VMEM((4, 4, 16, 256), BF16),
            pltpu.VMEM((3, 4, 16, 256), BF16),
            pltpu.VMEM((3, 4, 4, 16, 256), BF16),
            pltpu.VMEM((4, 4, 16, 256), BF16),
            pltpu.VMEM((3, 4, 16, 256), BF16),
            pltpu.VMEM((8, 16, 256), BF16),
            pltpu.VMEM((15, 16, 256), BF16),
            pltpu.VMEM((4, 16, 256), F32),
            dma((2, 8)), dma((2, 8)),
            dma((4,)), dma((4,)),
            dma((3,)), dma((3,)),
            dma((3, 4)), dma((3, 4)),
            dma((3,)), dma((3,)),
            dma((1,)), dma((1,)),
            dma((4,)), dma((4,)),
            dma((4, 3)), dma((4, 3)),
            dma((3,)), dma((3,)),
            dma((3,)), dma((3,)),
            dma((3,)), dma((3,)),
            dma((15,)), dma((15,)),
            dma((3,)), dma((3,)),
        ],
        compiler_params=pltpu.CompilerParams(
            collective_id=0, has_side_effects=True, vmem_limit_bytes=50 * 2**20
        ),
        name="decoder_crps_step",
    )(
        mesh_latent[0], grid_latent[0], senders, live_points.reshape(1, -1), target,
        w_send, w_recv, w_edge, w_out, gain.reshape(1, -1),
    )
    return (outs[0].reshape(PTS), outs[1], outs[2], outs[3], outs[4])


def solution(mesh):
    placed = (
        P("member", "band", None),
        P("member", "band", None),
        P("band", None),
        P(),
        P(None, "band"),
        P(),
        P(),
        P(),
        P(),
        P(),
    )
    return jax.shard_map(
        per_device,
        mesh=mesh,
        in_specs=placed,
        out_specs=(P("band"), P("band", None), P("band", None), P("band", None), P("band", None)),
        check_vma=False,
    )
```

time: 1680 us -> 75.7 us (0.05)
  waiting for transfers between devices: 1090 us -> 0 us
  blocking collectives: 495 us -> 0 us
  Pallas kernels: 0 us -> 65.6 us
  other arithmetic: 33.2 us -> 0.6 us
  local copies, waits for them, and re-layouts: 27.4 us -> 8.38 us
    reduce_scatter x2 -> x0, waiting for transfers between devices: 864 us -> none  [the longest x1 432 us: per_device(): lax.psum_scatter(summed[2], 'band', scatter_dimension=0, tiled=True)]
    unnamed x1 -> x0, blocking collectives: 419 us -> none
    psum x1 -> x0, waiting for transfers between devices: 213 us -> none  [per_device(): lax.psum(gradients[1].astype(jnp.bfloat16), 'member').astype(jnp.float32)]
    all_gather x1 -> x0, blocking collectives: 75.9 us -> none  [per_device(): fields = lax.all_gather(pred[None], 'member', axis=0, tiled=True)]
    pallas_call x0 -> x1, Pallas kernels: none -> 65.6 us  [per_device(): pl.pallas_call(kernel, out_shape=(shape((1, PTS), F32), shape((8, D), F32...]
    reduce_sum x5 -> x0, other arithmetic: 17.2 us -> none  [the longest x1 7.02 us: pair_terms(): abs_error = jnp.sum(root_error, axis=0) / count]
  transfers between devices with their start and end apart: 6 -> 0, of which waited for: 4 -> 0; matrix products, arithmetic and copies ran while one was open for 1% -> 0% of each run, Pallas kernels for 0% -> 0%
where the time goes in v1:
time: 75.7 us; the launch traced here: 75.3 us
  Pallas kernels  65.6 us (87%)
  local copies, waits for them, and re-layouts  8.38 us (11%)
    pallas_call x1, Pallas kernels, per_device(): pl.pallas_call(kernel, out_shape=(shape((1, PTS), F32), shape((8, D), F32...  65.6 us
    unnamed x22, local copies, waits for them, and re-layouts  8.38 us

profile of v1, /device:TPU:8, one launch (start us, length us, event | category | flops | bytes accessed | tf_op | source)
XLA Modules:
  0.0 75.3 jit_solution(6645687959945997912)
XLA Ops:
  0.6 0.0 copy-start.3
  0.6 1.1 %copy.16.wo_ref = bf16[512,100]{1,0:T(8,128)(2,1)S(1)} copy(bf16[512,100]{0,1:T(8,128)(2,1)} %param.18) | data formatting | bytes 204800 | tf_op args[8]
  1.7 0.0 copy-start.5
  1.7 0.0 copy-start.6
  1.7 0.0 copy-start.7
  1.8 0.9 %copy.15.send_ref = s32[320,3]{1,0:T(8,128)S(1)} copy(s32[320,3]{0,1:T(4,128)} %param.12) | data formatting | bytes 7680 | tf_op args[2]
  2.6 0.0 copy-done.3
  2.6 0.0 copy-done.5
  2.6 0.0 copy-done.6
  2.6 0.0 copy-done.7
  2.7 0.0 copy-start
  2.7 1.0 %copy-done = bf16[512,512]{1,0:T(8,128)(2,1)S(1)} copy-done((bf16[512,512]{1,0:T(8,128)(2,1)S(1)}, bf16[512,512]{1,0:T(8,128)(2,1)}, u32[]{:S(2)}) %copy-start) | copy-done | bytes 524312
  3.7 0.0 copy-start.1
  3.7 1.0 %copy-done.1 = bf16[512,512]{1,0:T(8,128)(2,1)S(1)} copy-done((bf16[512,512]{1,0:T(8,128)(2,1)S(1)}, bf16[512,512]{1,0:T(8,128)(2,1)}, u32[]{:S(2)}) %copy-start.1) | copy-done | bytes 524312
  4.7 0.0 copy-start.2
  4.7 1.0 %copy-done.2 = bf16[512,512]{1,0:T(8,128)(2,1)S(1)} copy-done((bf16[512,512]{1,0:T(8,128)(2,1)S(1)}, bf16[512,512]{1,0:T(8,128)(2,1)}, u32[]{:S(2)}) %copy-start.2) | copy-done | bytes 524312
  5.8 0.0 copy-start.4
  5.8 0.9 %copy-done.4 = bf16[1,128,512]{2,1,0:T(8,128)(2,1)S(1)} copy-done((bf16[1,128,512]{2,1,0:T(8,128)(2,1)S(1)}, bf16[1,128,512]{2,1,0:T(8,128)(2,1)}, u32[]{:S(2)}) %copy-start.4) | copy-done | bytes 131096
  6.7 65.6 %decoder_crps_step.1 = (f32[1,320]{1,0:T(1,128)S(1)}, f32[8,512]{1,0:T(8,128)S(1)}, f32[8,512]{1,0:T(8,128)S(1)}, f32[8,512]{1,0:T(8,128)S(1)}, f32[8,100]{1,0:T(8,128)S(1)}) custom-call(bf16[128,512]{1,0:T(8,128)(2,1)S(1)} %bitcast.5, bf16[320,512]{1,0:T(8,128)(2,1)S(1)} %bitcast.4, s32[320,3]{1,0:T(8,128)S(1)} %copy.15.send_ref, s32[1,64]{1,0:T(1,128)S(1)} %bitcast.7, ...), custom_call_target="tpu_custom_call" | custom-call | tf_op jit(solution)/shard_map/decoder_crps_step/pallas_call | solution.py:369
  72.3 0.6 reduce
  72.9 0.6 copy.21
  73.5 0.6 copy.22
  74.1 0.6 copy.23
  74.7 0.6 copy.24
Async XLA Ops:
  0.6 2.0 %copy-start.3 = (bf16[1,320,512]{2,1,0:T(8,128)(2,1)S(1)}, bf16[1,320,512]{2,1,0:T(8,128)(2,1)}, u32[]{:S(2)}) copy-start(bf16[1,320,512]{2,1,0:T(8,128)(2,1)} %param.11) | copy-start | bytes 983044
  1.7 0.9 %copy-start.5 = (bf16[100,320]{1,0:T(8,128)(2,1)S(1)}, bf16[100,320]{1,0:T(8,128)(2,1)}, u32[]{:S(2)}) copy-start(bf16[100,320]{1,0:T(8,128)(2,1)} %target_ref.1) | copy-start | bytes 192004
  1.7 0.9 %copy-start.6 = (f32[512]{0:T(512)S(1)}, f32[512]{0:T(512)}, u32[]{:S(2)}) copy-start(f32[512]{0:T(512)} %param.19) | copy-start | bytes 6148
  1.7 0.9 %copy-start.7 = (s32[64]{0:T(128)S(1)}, s32[64]{0:T(128)}, u32[]{:S(2)}) copy-start(s32[64]{0:T(128)} %param.13) | copy-start | bytes 772
  2.7 1.0 %copy-start = (bf16[512,512]{1,0:T(8,128)(2,1)S(1)}, bf16[512,512]{1,0:T(8,128)(2,1)}, u32[]{:S(2)}) copy-start(bf16[512,512]{1,0:T(8,128)(2,1)} %ws_ref.1) | copy-start | bytes 1572868
  3.7 1.0 %copy-start.1 = (bf16[512,512]{1,0:T(8,128)(2,1)S(1)}, bf16[512,512]{1,0:T(8,128)(2,1)}, u32[]{:S(2)}) copy-start(bf16[512,512]{1,0:T(8,128)(2,1)} %wr_ref.1) | copy-start | bytes 1572868
  4.7 1.0 %copy-start.2 = (bf16[512,512]{1,0:T(8,128)(2,1)S(1)}, bf16[512,512]{1,0:T(8,128)(2,1)}, u32[]{:S(2)}) copy-start(bf16[512,512]{1,0:T(8,128)(2,1)} %we_ref.1) | copy-start | bytes 1572868
  5.8 0.9 %copy-start.4 = (bf16[1,128,512]{2,1,0:T(8,128)(2,1)S(1)}, bf16[1,128,512]{2,1,0:T(8,128)(2,1)}, u32[]{:S(2)}) copy-start(bf16[1,128,512]{2,1,0:T(8,128)(2,1)} %param.10) | copy-start | bytes 393220

commit v2 on v1

v2 whole, which is shorter than its diff:
```python
import jax
import jax.numpy as jnp
from jax import lax
from jax.experimental import pallas as pl
from jax.experimental.pallas import tpu as pltpu
from jax.sharding import PartitionSpec as P

HALO = 32
SMOOTH_SQ = 0.0625
MESH = pl.DeviceIdType.MESH
F32 = jnp.float32
BF16 = jnp.bfloat16

D = 512
NCH = 4
PIECE_AT, PIECES = (0, 3, 5), (3, 2, 2)
SLOT_AT, SLOTS = (0, 2, 3), (2, 1, 1)
ORDER_Z = (8, 7, 9, 6, 10, 5, 11, 4, 12, 3, 13, 2, 14, 1, 15)
VMEM_LIMIT = 64 * 2**20 - 2**18
VARS = 100
PTS = 320
OWN = 128
ROWS = OWN + 2 * HALO
PACK = 256
TAIL = PTS - PACK
FOLD = 25


def dot(a, b, dims=((1,), (0,))):
    return lax.dot_general(a, b, (dims, ((), ())), preferred_element_type=F32)


def lanes_of(shape):
    return lax.broadcasted_iota(jnp.int32, shape, 1)


def rows_of(shape):
    return lax.broadcasted_iota(jnp.int32, shape, 0)


def pack_field(x):
    tail = x[PACK:]
    lane = lanes_of(tail.shape)
    inside = (lane >= VARS) & (lane < VARS + FOLD)
    parts = [jnp.where(inside, pltpu.roll(tail, VARS - FOLD * j, 1), 0.0) for j in range(4)]
    return x[:PACK] + jnp.concatenate(parts, axis=0)


def unpack_field(x):
    lane = lanes_of((TAIL, 128))
    tail = jnp.zeros((TAIL, 128), F32)
    for j in range(4):
        moved = pltpu.roll(x[TAIL * j : TAIL * (j + 1)], 128 - (VARS - FOLD * j), 1)
        tail = tail + jnp.where((lane >= FOLD * j) & (lane < FOLD * (j + 1)), moved, 0.0)
    main = jnp.where(lanes_of((PACK, 128)) < VARS, x, 0.0)
    return jnp.concatenate([main, tail], axis=0)


def kernel(
    mesh_hbm, grid_hbm, send_hbm, live_hbm, target_hbm, ws_hbm, wr_hbm, we_hbm, wo_hbm, gain_hbm,
    crow_z, final,
    mesh_ref, grid_ref, send_ref, live_ref, target_ref, ws_ref, wr_ref, we_ref, wo_ref, gain_ref,
    s_in, halo, wo, wpad, tpad, spad, onehot_t, slope_k, fields, crow,
    normed_t, agg_t, grid_t, mesh_t,
    part, part3, core_in, core_in3, summed, summed3, x_in1, x_in3, x_sum1, y_in1, y_in2, y_sum2, x_in2, slab, z_in,
    s_halo, r_halo, s_fz, r_fz, s_fy, r_fy, s_fzy, r_fzy, s_cy, r_cy, s_cz, r_cz,
    ok_far, s_core, r_core, s_x1, r_x1, s_y1, r_y1, s_y2, r_y2, s_x2, r_x2, s_z, r_z, s_g, r_g,
):
    member = lax.axis_index("member")
    band = lax.axis_index("band")
    zh, y = member // 4, member % 4
    x, zl, c = band // 16, (band // 2) % 8, band % 2
    z = zh * 8 + zl

    def dev(z_, y_, x_, c_):
        return ((z_ // 8) * 4 + y_, x_ * 16 + (z_ % 8) * 2 + c_)

    def z_peer(k):
        return dev((z + k) % 16, y, x, c)

    def y_peer(k):
        return dev(z, (y + k) % 4, x, c)

    def x_peer(k):
        return dev(z, y, (x + k) % 4, c)

    sibling = dev(z, y, x, 1 - c)
    other = (member, (band + 2 * c - 1 + 64) % 64)
    far = zl == 7 * c

    def rcopy(src, dst, ss, rs, to):
        return pltpu.make_async_remote_copy(
            src_ref=src, dst_ref=dst, send_sem=ss, recv_sem=rs, device_id=to, device_id_type=MESH
        )

    barrier = pltpu.get_barrier_semaphore()
    peers = [other] + [z_peer(k) for k in ORDER_Z]
    peers += [y_peer(k) for k in (1, 2, 3)] + [x_peer(k) for k in (1, 2, 3)] + [sibling]

    def across(k):
        return dev((z + 8) % 16, (y + k) % 4, x, c)

    def greet(p):
        pl.semaphore_signal(barrier, inc=1, device_id=p, device_id_type=MESH)

    for p in peers:
        greet(p)

    hbm = (mesh_hbm, ws_hbm, grid_hbm, wr_hbm, send_hbm, target_hbm, live_hbm, gain_hbm, wo_hbm, we_hbm)
    near = (mesh_ref, ws_ref, grid_ref, wr_ref, send_ref, target_ref, live_ref, gain_ref, wo_ref, we_ref)
    loads = [pltpu.make_async_copy(a, b, s_in.at[i]) for i, (a, b) in enumerate(zip(hbm, near))]
    for cp in loads:
        cp.start()

    sends, pending = [], {}

    def start(*copies):
        for cp in copies:
            cp.start()
            sends.append(cp)
            pending[id(cp)] = cp

    def arrive(*copies):
        for cp in copies:
            cp.wait_recv()
            del pending[id(cp)]

    def finish():
        arrive(*list(pending.values()))
        for cp in sends:
            cp.wait_send()

    loads[0].wait()
    loads[1].wait()
    sent_own = dot(mesh_ref[...], ws_ref[...])
    loads[2].wait()
    loads[3].wait()
    recv_rows = dot(grid_ref[...], wr_ref[...])
    for cp in loads[4:]:
        cp.wait()
    wpad[...] = jnp.zeros(wpad.shape, F32)
    wpad[:VARS] = wo_ref[...].astype(F32)
    wo[...] = wpad[...].astype(BF16)
    tpad[...] = jnp.zeros(tpad.shape, F32)
    tpad[:VARS, :PTS] = target_ref[...].astype(F32)
    truth = pack_field(jnp.transpose(tpad[...])[:PTS])
    spad[...] = jnp.zeros(spad.shape, F32)
    spad[:3, :PTS] = send_ref[...].astype(F32)
    senders = jnp.transpose(spad[...])[:PTS].astype(jnp.int32)

    low_at = jnp.where(c == 0, OWN, OWN + HALO)
    high_at = jnp.where(c == 0, OWN + HALO, OWN)

    def moved(s):
        return jnp.where(s < HALO, s + low_at, jnp.where(s < HALO + OWN, s - HALO, s - (HALO + OWN) + high_at))

    index = moved(senders)
    index_t = moved(send_ref[...])
    for k in range(3):
        hit = rows_of((ROWS, PTS)) == index_t[k : k + 1, :]
        onehot_t[k] = jnp.where(hit, 1.0, 0.0).astype(BF16)
    live = live_ref[...]
    lane64 = lanes_of(live.shape)
    count = jnp.sum(jnp.where(lane64 == band, live, 0).astype(F32), axis=1, keepdims=True)
    total = jnp.sum(live.astype(F32), axis=1, keepdims=True)
    scale = 1.0 / (total * VARS)
    row = rows_of((PACK, 128))
    lane = lanes_of((PACK, 128))
    point = jnp.where(lane < VARS, row, PACK + row % TAIL)
    mask = jnp.where((lane < VARS + FOLD) & (point.astype(F32) < count), 1.0, 0.0)

    pl.semaphore_wait(barrier, len(peers))

    @pl.when(far)
    def _():
        pl.semaphore_signal(ok_far, inc=1, device_id=z_peer(8), device_id_type=MESH)


    facing = pl.multiple_of((OWN - HALO) * c, HALO)
    behind = pl.multiple_of((OWN - HALO) * (1 - c), HALO)
    halo_copies = []
    for i in range(2):
        for j in range(4):
            n = i * 4 + j
            cols = pl.ds(128 * j, 128)
            src = mesh_ref.at[pl.ds(pl.multiple_of(facing + 16 * i, 16), 16), cols]
            halo_copies.append(rcopy(src, halo.at[0, pl.ds(16 * i, 16), cols], s_halo.at[n], r_halo.at[n], other))
    halo_copies.append(rcopy(mesh_ref.at[pl.ds(behind, HALO)], halo.at[1], s_halo.at[8], r_halo.at[8], sibling))
    start(*halo_copies)
    arrive(*halo_copies)
    polar = (band == 0) | (band == 63)
    outer = jnp.where(polar, 0.0, halo[0].astype(F32)).astype(BF16)
    edge_rows = jnp.concatenate([outer, halo[1]], axis=0)
    sent_edge = dot(edge_rows, ws_ref[...])
    sent = jnp.concatenate([sent_own, sent_edge], axis=0).astype(BF16)

    agg = jnp.zeros((PTS, D), F32)
    for k in range(3):
        hit = lanes_of((PTS, ROWS)) == index[:, k : k + 1]
        pre = dot(jnp.where(hit, 1.0, 0.0).astype(BF16), sent) + recv_rows
        sig = 0.5 * jnp.tanh(0.5 * pre) + 0.5
        act = pre * sig
        agg = agg + act
        slope_k[k] = sig + act * (1.0 - sig)
    agg_in = agg.astype(BF16)
    hidden = grid_ref[...].astype(F32) + dot(agg_in, we_ref[...])
    inv_rms = lax.rsqrt(jnp.mean(hidden * hidden, axis=1, keepdims=True) + 1e-05)
    gain = gain_ref[...]
    normed = (hidden * inv_rms * gain).astype(BF16)
    pred = dot(normed, wo[...], ((1,), (1,)))
    fields[0, 0] = pack_field(pred).astype(BF16)

    def rows(n):
        return pl.ds(PACK // NCH * n, PACK // NCH)

    fz = [
        rcopy(fields.at[0, 0, rows(n)], fields.at[1, 0, rows(n)], s_fz.at[n], r_fz.at[n], z_peer(8))
        for n in range(NCH)
    ]
    fy = [
        rcopy(fields.at[0, 0], fields.at[0, k], s_fy.at[k - 1], r_fy.at[k - 1], y_peer(k))
        for k in (1, 2, 3)
    ]
    fzy = [
        [
            rcopy(
                fields.at[1, 0, rows(n)], fields.at[1, k, rows(n)], s_fzy.at[k - 1, n], r_fzy.at[k - 1, n], y_peer(k)
            )
            for k in (1, 2, 3)
        ]
        for n in range(NCH)
    ]
    straight = [
        rcopy(fields.at[0, 0, rows(n)], fields.at[1, k, rows(n)], s_fzy.at[k - 1, n], r_fzy.at[k - 1, n], across(k))
        for n in range(NCH)
        for k in (1, 2, 3)
    ]
    start(*fz)

    @pl.when(far)
    def _():
        pl.semaphore_wait(ok_far, 1)
        for cp in straight:
            cp.start()

    start(*fy)
    normed_t[...] = jnp.transpose(normed)
    agg_t[...] = jnp.transpose(agg_in)
    grid_t[...] = jnp.transpose(grid_ref[...])
    mesh_t[:, :OWN] = jnp.transpose(mesh_ref[...])
    mesh_t[:, OWN:] = jnp.transpose(edge_rows)

    own = fields[0, 0].astype(F32)
    error = own - truth
    error_sq = error * error + SMOOTH_SQ
    error_inv = lax.rsqrt(error_sq)
    pair_slope = jnp.zeros((PACK, 128), F32)
    spread = jnp.full((PACK, 128), 0.25, F32)

    def pair(h, k, pair_slope, spread):
        differ = own - fields[h, k].astype(F32)
        sq = differ * differ + SMOOTH_SQ
        inv = lax.rsqrt(sq)
        return pair_slope + differ * inv, spread + sq * inv

    for k in (1, 2, 3):
        arrive(fy[k - 1])
        pair_slope, spread = pair(0, k, pair_slope, spread)
    for n in range(NCH):
        arrive(fz[n])

        @pl.when(jnp.logical_not(far))
        def _(n=n):
            for cp in fzy[n]:
                cp.start()

        for cp in fzy[n]:
            sends.append(cp)
            pending[id(cp)] = cp
    pair_slope, spread = pair(1, 0, pair_slope, spread)
    for k in (1, 2, 3):
        for n in range(NCH):
            arrive(fzy[n][k - 1])
        pair_slope, spread = pair(1, k, pair_slope, spread)

    field_grad = (error * error_inv * 0.125 - pair_slope * (1.0 / 56.0)) * (mask * scale)
    grad16 = unpack_field(field_grad).astype(BF16)


    def store_part(q, full):
        for t in range(2):
            halves = [full[:, 256 * t + 128 * i : 256 * t + 128 * (i + 1)].reshape(64, 8, 128) for i in range(2)]
            block = jnp.concatenate(halves, axis=1).astype(BF16).reshape(4, 4, 2, 2, 16, 128)
            for p in range(2):
                for cc in range(2):
                    part[cc, q, t, p] = block[:, :, p, cc]

    def store_head(full):
        bands = full.reshape(4, 4, 2, 2, 8, 128)
        for t in range(2):
            for p in range(2):
                for cc in range(2):
                    two = jnp.concatenate([bands[:, 2 * t, p, cc], bands[:, 2 * t + 1, p, cc]], axis=1)
                    part3[cc, p, t] = two.astype(BF16)

    core = [rcopy(part.at[1 - c, q], core_in.at[q], s_core.at[q], r_core.at[q], sibling) for q in range(3)]
    core.append(rcopy(part3.at[1 - c], core_in3, s_core.at[3], r_core.at[3], sibling))
    d_normed = dot(grad16, wo[...])
    store_head(dot(normed_t[...], grad16))
    start(core[3])
    gained = d_normed * gain
    mean = jnp.mean(gained * hidden, axis=1, keepdims=True)
    d_hidden = (inv_rms * gained - hidden * (inv_rms * inv_rms * inv_rms * mean)).astype(BF16)
    d_agg = dot(d_hidden, we_ref[...], ((1,), (1,)))
    store_part(2, dot(agg_t[...], d_hidden))
    start(core[2])
    d_recv = jnp.zeros((PTS, D), F32)
    d_sent = jnp.zeros((ROWS, D), F32)
    for k in range(3):
        d_pre = d_agg * slope_k[k]
        d_recv = d_recv + d_pre
        d_sent = d_sent + dot(onehot_t[k], d_pre.astype(BF16))
    store_part(1, dot(grid_t[...], d_recv.astype(BF16)))
    start(core[1])
    store_part(0, dot(mesh_t[...], d_sent.astype(BF16)))
    start(core[0])

    crps = (error_sq * error_inv * 0.125 - spread * (1.0 / 112.0)) * mask
    crps_hi = crps.astype(BF16)
    crps_lo = (crps - crps_hi.astype(F32)).astype(BF16)
    lane8 = lanes_of((8, 128))
    take_main = jnp.where(lane8 < VARS, 1.0, 0.0).astype(BF16)
    take_tail = jnp.where((lane8 >= VARS) & (lane8 < VARS + FOLD), 1.0, 0.0).astype(BF16)
    wide = ((1,), (1,))
    main = dot(take_main, crps_hi, wide) + dot(take_main, crps_lo, wide)
    tail = dot(take_tail, crps_hi, wide) + dot(take_tail, crps_lo, wide)
    tail = tail[:, :128] + tail[:, 128:]
    tail = tail + pltpu.roll(tail, 64, 1)
    crow[0, :, :256] = main
    crow[0, :, 256:] = tail
    cy = [rcopy(crow.at[0], crow.at[k], s_cy.at[k - 1], r_cy.at[k - 1], y_peer(k)) for k in (1, 2, 3)]
    start(*cy)

    def x1_copy(k, q):
        to = (x + k) % 4
        src = summed3.at[:, :, to] if q == 3 else summed.at[q, :, :, to, pl.ds(0, 2)]
        dst = x_in3.at[k - 1] if q == 3 else x_in1.at[q, k - 1]
        return rcopy(src, dst, s_x1.at[q, k - 1], r_x1.at[q, k - 1], x_peer(k))

    def y2_copy(k, q):
        to = (y + k) % 4
        src = summed.at[q, to % 2, to // 2, :, pl.ds(2, 2)]
        return rcopy(src, y_in2.at[q, k - 1], s_y2.at[q, k - 1], r_y2.at[q, k - 1], y_peer(k))

    x1 = [[x1_copy(k, q) for k in (1, 2, 3)] for q in range(4)]
    y2 = [[y2_copy(k, q) for k in (1, 2, 3)] for q in range(3)]

    def add(a, b):
        return (a.astype(F32) + b.astype(F32)).astype(BF16)

    for q in (3, 2, 1, 0):
        arrive(core[q])
        if q == 3:
            summed3[...] = add(part3[c], core_in3[...])
            start(*x1[q])
        else:
            summed[q] = add(part[c, q], core_in[q])
            for k in (1, 0, 2):
                start(x1[q][k], y2[q][k])

    arrive(*cy)
    crow_z[0] = (crow[0] + crow[1]) + (crow[2] + crow[3])
    cz = rcopy(crow_z.at[0], crow_z.at[1], s_cz.at[0], r_cz.at[0], z_peer(8))
    start(cz)

    def add4(a, b0, b1, b2):
        return ((a.astype(F32) + b0.astype(F32)) + (b1.astype(F32) + b2.astype(F32))).astype(BF16)

    def y1_copy(k, g):
        n = pl.ds(PIECE_AT[g], PIECES[g])
        return rcopy(x_sum1.at[(y + k) % 4, n], y_in1.at[k - 1, n], s_y1.at[g, k - 1], r_y1.at[g, k - 1], y_peer(k))

    def x2_copy(k, q):
        return rcopy(y_sum2.at[(x + k) % 4, q], x_in2.at[q, k - 1], s_x2.at[q, k - 1], r_x2.at[q, k - 1], x_peer(k))

    y1 = [[y1_copy(k, g) for k in (1, 2, 3)] for g in range(3)]
    x2 = [[x2_copy(k, q) for k in (1, 2, 3)] for q in range(3)]
    for q in (3, 2, 1, 0):
        arrive(*x1[q])
        if q == 3:
            head = add4(summed3[:, :, x], x_in3[0], x_in3[1], x_in3[2])
            for p in range(2):
                for t in range(2):
                    x_sum1[2 * p + t, 0] = head[p, t]
            continue
        g = 2 - q
        at = PIECE_AT[g] + PIECES[g] - 2
        body = add4(summed[q, :, :, x, 0:2], x_in1[q, 0], x_in1[q, 1], x_in1[q, 2])
        for p in range(2):
            for t in range(2):
                x_sum1[2 * p + t, at : at + 2] = body[t, p]
        start(y1[g][1], y1[g][0], y1[g][2])
        arrive(*y2[q])
        y_sum2[:, q] = add4(summed[q, y % 2, y // 2, :, 2:4], y_in2[q, 0], y_in2[q, 1], y_in2[q, 2])
        start(x2[q][1], x2[q][0], x2[q][2])

    away = (zl + y // 2) % 2
    owner = away == 0

    def z_copy(j, g):
        k = 2 * j + away
        n = pl.ds(SLOT_AT[g], SLOTS[g])
        return rcopy(slab.at[((z + k) % 8) // 2, n], z_in.at[k, n], s_z.at[g, j], r_z.at[g, k], z_peer(k))

    def z_arrived(k, g):
        n = pl.ds(SLOT_AT[g], SLOTS[g])
        rcopy(slab.at[0, n], z_in.at[k, n], s_z.at[g, 0], r_z.at[g, k], z_peer(8)).wait_recv()

    def g_copy(k, g):
        n = pl.ds(SLOT_AT[g], SLOTS[g])
        return rcopy(final.at[y % 2, n], final.at[y % 2, n], s_g.at[g, k - 1], r_g.at[g, y % 2], y_peer(k))

    for g in range(3):
        q = 2 - g
        lo, hi = SLOT_AT[g], SLOT_AT[g] + SLOTS[g]
        arrive(*y1[g])
        n = pl.ds(PIECE_AT[g], PIECES[g])
        done1 = add4(x_sum1[y, n], y_in1[0, n], y_in1[1, n], y_in1[2, n])
        if g == 0:
            for h in range(4):
                slab[h, 0] = done1[0]
        for h in range(2):
            slab[h, hi - 1] = done1[PIECES[g] - 2 + h]
        arrive(*x2[q])
        done2 = add4(y_sum2[x, q], x_in2[q, 0], x_in2[q, 1], x_in2[q, 2])
        for h in range(2):
            slab[2 + h, hi - 1] = done2[h]
        for j in (4, 3, 5, 2, 6, 1, 7):
            z_copy(j, g).start()

        @pl.when(away == 1)
        def _(g=g):
            z_copy(0, g).start()


    @pl.when(owner)
    def _():
        for g in range(3):
            n = pl.ds(SLOT_AT[g], SLOTS[g])
            acc = slab[zl // 2, n].astype(F32)
            for k in (1, 15, 2, 14, 3, 13, 4, 12, 5, 11, 6, 10, 7, 9, 8):
                z_arrived(k, g)
                acc = acc + z_in[k, n].astype(F32)
            final[y % 2, n] = acc
            for k in (2, 1, 3):
                g_copy(k, g).start()

    arrive(cz)
    for t in range(2):

        @pl.when(jnp.logical_not(owner & (y % 2 == t)))
        def _(t=t):
            for g in range(3):
                n = pl.ds(SLOT_AT[g], SLOTS[g])
                rcopy(final.at[t, n], final.at[t, n], s_g.at[g, 0], r_g.at[g, t], z_peer(8)).wait_recv()

    @pl.when(owner)
    def _():
        for g in range(3):
            for k in (1, 2, 3):
                g_copy(k, g).wait_send()

    @pl.when(away == 1)
    def _():
        for g in range(3):
            z_copy(0, g).wait_send()

    for g in range(3):
        for j in range(1, 8):
            z_copy(j, g).wait_send()
    finish()


def unpack(crow_ref, final_ref, crps_out, gs_out, gr_out, ge_out, go_out):
    zl = (lax.axis_index("band") // 2) % 8
    crps_out[...] = (crow_ref[0] + crow_ref[1])[0, :PTS]
    for q, out in ((0, gs_out), (1, gr_out), (2, ge_out)):
        for t in range(2):
            got = final_ref[t, 3 - q]
            out[:, 256 * t : 256 * t + 128] = got[:8]
            out[:, 256 * t + 128 : 256 * t + 256] = got[8:]
    got = final_ref[zl // 4, 0]
    go_out[...] = jnp.where((zl // 2) % 2 == 0, got[:8, :VARS], got[8:, :VARS])


def per_device(mesh_latent, grid_latent, senders, live_points, target, w_send, w_recv, w_edge, w_out, gain):
    vmem = pl.BlockSpec(memory_space=pltpu.VMEM)
    dma = pltpu.SemaphoreType.DMA
    shape = jax.ShapeDtypeStruct
    args = (
        mesh_latent[0], grid_latent[0], senders.T, live_points.reshape(1, -1), target,
        w_send, w_recv, w_edge, w_out.T, gain.reshape(1, -1),
    )
    crow, final = pl.pallas_call(
        kernel,
        out_shape=(shape((2, 8, 384), F32), shape((2, 4, 16, 128), F32)),
        in_specs=[pl.BlockSpec(memory_space=pltpu.HBM)] * 10,
        out_specs=[vmem] * 2,
        scratch_shapes=[pltpu.VMEM(a.shape, a.dtype) for a in args]
        + [
            dma((10,)),
            pltpu.VMEM((2, HALO, D), BF16),
            pltpu.VMEM((128, D), BF16),
            pltpu.VMEM((128, D), F32),
            pltpu.VMEM((128, 384), F32),
            pltpu.VMEM((128, 384), F32),
            pltpu.VMEM((3, ROWS, PTS), BF16),
            pltpu.VMEM((3, PTS, D), F32),
            pltpu.VMEM((2, 4, PACK, 128), BF16),
            pltpu.VMEM((4, 8, 384), F32),
            pltpu.VMEM((D, PTS), BF16),
            pltpu.VMEM((D, PTS), BF16),
            pltpu.VMEM((D, PTS), BF16),
            pltpu.VMEM((D, ROWS), BF16),
            pltpu.VMEM((2, 3, 2, 2, 4, 4, 16, 128), BF16),
            pltpu.VMEM((2, 2, 2, 4, 16, 128), BF16),
            pltpu.VMEM((3, 2, 2, 4, 4, 16, 128), BF16),
            pltpu.VMEM((2, 2, 4, 16, 128), BF16),
            pltpu.VMEM((3, 2, 2, 4, 4, 16, 128), BF16),
            pltpu.VMEM((2, 2, 4, 16, 128), BF16),
            pltpu.VMEM((3, 3, 2, 2, 2, 16, 128), BF16),
            pltpu.VMEM((3, 2, 2, 16, 128), BF16),
            pltpu.VMEM((4, 7, 16, 128), BF16),
            pltpu.VMEM((3, 7, 16, 128), BF16),
            pltpu.VMEM((3, 3, 4, 2, 16, 128), BF16),
            pltpu.VMEM((4, 3, 2, 16, 128), BF16),
            pltpu.VMEM((3, 3, 2, 16, 128), BF16),
            pltpu.VMEM((4, 4, 16, 128), BF16),
            pltpu.VMEM((16, 4, 16, 128), BF16),
            dma((9,)), dma((9,)),
            dma((NCH,)), dma((NCH,)),
            dma((3,)), dma((3,)),
            dma((3, NCH)), dma((3, NCH)),
            dma((3,)), dma((3,)),
            dma((1,)), dma((1,)),
            pltpu.SemaphoreType.REGULAR,
            dma((4,)), dma((4,)),
            dma((4, 3)), dma((4, 3)),
            dma((3, 3)), dma((3, 3)),
            dma((3, 3)), dma((3, 3)),
            dma((3, 3)), dma((3, 3)),
            dma((3, 8)), dma((3, 16)),
            dma((3, 3)), dma((3, 2)),
        ],
        compiler_params=pltpu.CompilerParams(
            collective_id=0, has_side_effects=True, vmem_limit_bytes=VMEM_LIMIT
        ),
        name="decoder_crps_step",
    )(*args)
    outs = pl.pallas_call(
        unpack,
        out_shape=(
            shape((PTS,), F32),
            shape((8, D), F32),
            shape((8, D), F32),
            shape((8, D), F32),
            shape((8, VARS), F32),
        ),
        in_specs=[vmem] * 2,
        out_specs=[vmem] * 5,
        compiler_params=pltpu.CompilerParams(vmem_limit_bytes=VMEM_LIMIT),
        name="unpack",
    )(crow, final)
    return outs


def solution(mesh):
    placed = (
        P("member", "band", None),
        P("member", "band", None),
        P("band", None),
        P(),
        P(None, "band"),
        P(),
        P(),
        P(),
        P(),
        P(),
    )
    return jax.shard_map(
        per_device,
        mesh=mesh,
        in_specs=placed,
        out_specs=(P("band"), P("band", None), P("band", None), P("band", None), P("band", None)),
        check_vma=False,
    )
```

time: 75.7 us -> 65.2 us (0.86)
  the two profiles are of different devices: /device:TPU:8 before, /device:TPU:32 now
where the time goes in v2:
time: 65.2 us; the launch traced here: 65 us
  Pallas kernels  64.4 us (99%)
    pallas_call x1, Pallas kernels, per_device(): pl.pallas_call(kernel, out_shape=(shape((2, 8, 384), F32), shape((2, 4, 1...  62.9 us
    pallas_call x1, Pallas kernels, per_device(): pl.pallas_call(unpack, out_shape=(shape((PTS,), F32), shape((8, D), F32),...  1.49 us

profile of v2, /device:TPU:32, one launch (start us, length us, event | category | flops | bytes accessed | tf_op | source)
XLA Modules:
  0.0 65.0 jit_solution(12884507155416062009)
XLA Ops:
  0.6 62.9 %decoder_crps_step.1 = (f32[2,8,384]{2,1,0:T(8,128)}, f32[2,4,16,128]{3,2,1,0:T(8,128)}) custom-call(bf16[128,512]{1,0:T(8,128)(2,1)} %bitcast.7, bf16[320,512]{1,0:T(8,128)(2,1)} %bitcast.6, s32[3,320]{1,0:T(4,128)} %bitcast.9, s32[1,64]{1,0:T(1,128)} %bitcast.11, bf16[100,320]{1,0:T(8,128)(2,1)} %target_hbm.1, bf16[512,512]{1,0:T(8,128)(2,1)} %ws_hbm.1, ...), custom_call_target="tpu_custom_call" | custom-call | tf_op jit(solution)/shard_map/decoder_crps_step/pallas_call | solution.py:504
  63.5 1.5 %unpack.1 = (f32[320]{0:T(512)}, f32[8,512]{1,0:T(8,128)}, f32[8,512]{1,0:T(8,128)}, f32[8,512]{1,0:T(8,128)}, f32[8,100]{1,0:T(8,128)}) custom-call(f32[2,8,384]{2,1,0:T(8,128)} %get-tuple-element.7.crow_ref, f32[2,4,16,128]{3,2,1,0:T(8,128)} %get-tuple-element.8.final_ref), custom_call_target="tpu_custom_call" | custom-call | tf_op jit(solution)/shard_map/unpack/pallas_call | solution.py:560

commit v3 on v2

--- a/solution.py
+++ b/solution.py
@@ -13,6 +13,7 @@
 
 D = 512
 NCH = 4
+LEG = 3
 PIECE_AT, PIECES = (0, 3, 5), (3, 2, 2)
 SLOT_AT, SLOTS = (0, 2, 3), (2, 1, 1)
 ORDER_Z = (8, 7, 9, 6, 10, 5, 11, 4, 12, 3, 13, 2, 14, 1, 15)
@@ -60,11 +61,11 @@
     mesh_hbm, grid_hbm, send_hbm, live_hbm, target_hbm, ws_hbm, wr_hbm, we_hbm, wo_hbm, gain_hbm,
     crow_z, final,
     mesh_ref, grid_ref, send_ref, live_ref, target_ref, ws_ref, wr_ref, we_ref, wo_ref, gain_ref,
-    s_in, halo, wo, wpad, tpad, spad, onehot_t, slope_k, fields, crow,
+    s_in, halo, held, wo, wpad, tpad, spad, onehot_t, slope_k, fields, crow,
     normed_t, agg_t, grid_t, mesh_t,
     part, part3, core_in, core_in3, summed, summed3, x_in1, x_in3, x_sum1, y_in1, y_in2, y_sum2, x_in2, slab, z_in,
     s_halo, r_halo, s_fz, r_fz, s_fy, r_fy, s_fzy, r_fzy, s_cy, r_cy, s_cz, r_cz,
-    ok_far, s_core, r_core, s_x1, r_x1, s_y1, r_y1, s_y2, r_y2, s_x2, r_x2, s_z, r_z, s_g, r_g,
+    ok_z, ok_far, s_held, r_held, s_core, r_core, s_x1, r_x1, s_y1, r_y1, s_y2, r_y2, s_x2, r_x2, s_z, r_z, s_g, r_g,
 ):
     member = lax.axis_index("member")
     band = lax.axis_index("band")
@@ -87,6 +88,10 @@
     sibling = dev(z, y, x, 1 - c)
     other = (member, (band + 2 * c - 1 + 64) % 64)
     far = zl == 7 * c
+    near = jnp.logical_not(far)
+    relay = zl == LEG + (7 - 2 * LEG) * c
+    beyond = (member, (band + (2 * LEG + 1) * (2 * c - 1) + 64) % 64)
+    to_relay = z_peer(LEG * (1 - 2 * c) + 16)
 
     def rcopy(src, dst, ss, rs, to):
         return pltpu.make_async_remote_copy(
@@ -94,8 +99,6 @@
         )
 
     barrier = pltpu.get_barrier_semaphore()
-    peers = [other] + [z_peer(k) for k in ORDER_Z]
-    peers += [y_peer(k) for k in (1, 2, 3)] + [x_peer(k) for k in (1, 2, 3)] + [sibling]
 
     def across(k):
         return dev((z + 8) % 16, (y + k) % 4, x, c)
@@ -103,12 +106,22 @@
     def greet(p):
         pl.semaphore_signal(barrier, inc=1, device_id=p, device_id_type=MESH)
 
+    @pl.when(far)
+    def _():
+        greet(beyond)
+
+    @pl.when(near)
+    def _():
+        greet(other)
+
+    peers = [z_peer(k) for k in (4, 12, 3, 13, 2, 14, 1, 15)]
+    peers += [y_peer(k) for k in (2, 1, 3)] + [x_peer(k) for k in (2, 1, 3)] + [sibling]
     for p in peers:
         greet(p)
 
     hbm = (mesh_hbm, ws_hbm, grid_hbm, wr_hbm, send_hbm, target_hbm, live_hbm, gain_hbm, wo_hbm, we_hbm)
-    near = (mesh_ref, ws_ref, grid_ref, wr_ref, send_ref, target_ref, live_ref, gain_ref, wo_ref, we_ref)
-    loads = [pltpu.make_async_copy(a, b, s_in.at[i]) for i, (a, b) in enumerate(zip(hbm, near))]
+    here = (mesh_ref, ws_ref, grid_ref, wr_ref, send_ref, target_ref, live_ref, gain_ref, wo_ref, we_ref)
+    loads = [pltpu.make_async_copy(a, b, s_in.at[i]) for i, (a, b) in enumerate(zip(hbm, here))]
     for cp in loads:
         cp.start()
 
@@ -136,6 +149,38 @@
     loads[2].wait()
     loads[3].wait()
     recv_rows = dot(grid_ref[...], wr_ref[...])
+    pl.semaphore_wait(barrier, len(peers) + jnp.where(near, 1, 0) + jnp.where(relay, 1, 0))
+    for k in (4, 12):
+        pl.semaphore_signal(ok_z, inc=1, device_id=z_peer(k), device_id_type=MESH)
+
+    facing = pl.multiple_of((OWN - HALO) * c, HALO)
+    behind = pl.multiple_of((OWN - HALO) * (1 - c), HALO)
+    tiles = [(i, j) for i in range(2) for j in range(4)]
+
+    def tile(ref, n, base=0):
+        i, j = tiles[n]
+        return ref.at[pl.ds(pl.multiple_of(base + 16 * i, 16), 16), pl.ds(128 * j, 128)]
+
+    direct, first_leg, second_leg = [], [], []
+    for n in range(8):
+        mine = tile(mesh_ref, n, facing)
+        direct.append(rcopy(mine, tile(halo.at[0], n), s_halo.at[n], r_halo.at[n], other))
+        first_leg.append(rcopy(mine, tile(held, n), s_halo.at[n], r_held.at[n], to_relay))
+        second_leg.append(rcopy(tile(held, n), tile(halo.at[0], n), s_held.at[n], r_halo.at[n], beyond))
+
+    @pl.when(far)
+    def _():
+        for cp in first_leg:
+            cp.start()
+
+    @pl.when(near)
+    def _():
+        for cp in direct:
+            cp.start()
+
+    close = rcopy(mesh_ref.at[pl.ds(behind, HALO)], halo.at[1], s_halo.at[8], r_halo.at[8], sibling)
+    start(close)
+
     for cp in loads[4:]:
         cp.wait()
     wpad[...] = jnp.zeros(wpad.shape, F32)
@@ -169,25 +214,21 @@
     point = jnp.where(lane < VARS, row, PACK + row % TAIL)
     mask = jnp.where((lane < VARS + FOLD) & (point.astype(F32) < count), 1.0, 0.0)
 
-    pl.semaphore_wait(barrier, len(peers))
-
     @pl.when(far)
     def _():
-        pl.semaphore_signal(ok_far, inc=1, device_id=z_peer(8), device_id_type=MESH)
-
-
-    facing = pl.multiple_of((OWN - HALO) * c, HALO)
-    behind = pl.multiple_of((OWN - HALO) * (1 - c), HALO)
-    halo_copies = []
-    for i in range(2):
-        for j in range(4):
-            n = i * 4 + j
-            cols = pl.ds(128 * j, 128)
-            src = mesh_ref.at[pl.ds(pl.multiple_of(facing + 16 * i, 16), 16), cols]
-            halo_copies.append(rcopy(src, halo.at[0, pl.ds(16 * i, 16), cols], s_halo.at[n], r_halo.at[n], other))
-    halo_copies.append(rcopy(mesh_ref.at[pl.ds(behind, HALO)], halo.at[1], s_halo.at[8], r_halo.at[8], sibling))
-    start(*halo_copies)
-    arrive(*halo_copies)
+        pl.semaphore_wait(ok_z, 2)
+        for k in (2, 1, 3):
+            pl.semaphore_signal(ok_far, inc=1, device_id=y_peer(k), device_id_type=MESH)
+
+    @pl.when(relay)
+    def _():
+        for n in range(8):
+            first_leg[n].wait_recv()
+            second_leg[n].start()
+
+    arrive(close)
+    for cp in direct:
+        cp.wait_recv()
     polar = (band == 0) | (band == 63)
     outer = jnp.where(polar, 0.0, halo[0].astype(F32)).astype(BF16)
     edge_rows = jnp.concatenate([outer, halo[1]], axis=0)
@@ -233,13 +274,18 @@
     straight = [
         rcopy(fields.at[0, 0, rows(n)], fields.at[1, k, rows(n)], s_fzy.at[k - 1, n], r_fzy.at[k - 1, n], across(k))
         for n in range(NCH)
-        for k in (1, 2, 3)
+        for k in (2,)
     ]
+
+    @pl.when(near)
+    def _():
+        pl.semaphore_wait(ok_z, 2)
+
     start(*fz)
 
     @pl.when(far)
     def _():
-        pl.semaphore_wait(ok_far, 1)
+        pl.semaphore_wait(ok_far, 3)
         for cp in straight:
             cp.start()
 
@@ -269,10 +315,12 @@
     for n in range(NCH):
         arrive(fz[n])
 
-        @pl.when(jnp.logical_not(far))
+        fzy[n][0].start()
+        fzy[n][2].start()
+
+        @pl.when(near)
         def _(n=n):
-            for cp in fzy[n]:
-                cp.start()
+            fzy[n][1].start()
 
         for cp in fzy[n]:
             sends.append(cp)
@@ -478,6 +526,14 @@
     for g in range(3):
         for j in range(1, 8):
             z_copy(j, g).wait_send()
+    for cp in direct:
+        cp.wait_send()
+
+    @pl.when(relay)
+    def _():
+        for cp in second_leg:
+            cp.wait_send()
+
     finish()
 
 
@@ -510,6 +566,7 @@
         + [
             dma((10,)),
             pltpu.VMEM((2, HALO, D), BF16),
+            pltpu.VMEM((HALO, D), BF16),
             pltpu.VMEM((128, D), BF16),
             pltpu.VMEM((128, D), F32),
             pltpu.VMEM((128, 384), F32),
@@ -543,7 +600,8 @@
             dma((3, NCH)), dma((3, NCH)),
             dma((3,)), dma((3,)),
             dma((1,)), dma((1,)),
-            pltpu.SemaphoreType.REGULAR,
+            pltpu.SemaphoreType.REGULAR, pltpu.SemaphoreType.REGULAR,
+            dma((8,)), dma((8,)),
             dma((4,)), dma((4,)),
             dma((4, 3)), dma((4, 3)),
             dma((3, 3)), dma((3, 3)),

time: 65.2 us -> 63.4 us (0.972)
  the two profiles are of different devices: /device:TPU:32 before, /device:TPU:8 now
where the time goes in v3:
time: 63.4 us; the launch traced here: 63.2 us
  Pallas kernels  62.5 us (99%)
  between operations  0.64 us (1%)
    pallas_call x1, Pallas kernels, per_device(): pl.pallas_call(kernel, out_shape=(shape((2, 8, 384), F32), shape((2, 4, 1...  61.1 us
    pallas_call x1, Pallas kernels, per_device(): pl.pallas_call(unpack, out_shape=(shape((PTS,), F32), shape((8, D), F32),...  1.49 us

profile of v3, /device:TPU:8, one launch (start us, length us, event | category | flops | bytes accessed | tf_op | source)
XLA Modules:
  0.0 63.2 jit_solution(6846591177147379606)
XLA Ops:
  0.6 61.1 %decoder_crps_step.1 = (f32[2,8,384]{2,1,0:T(8,128)}, f32[2,4,16,128]{3,2,1,0:T(8,128)}) custom-call(bf16[128,512]{1,0:T(8,128)(2,1)} %bitcast.7, bf16[320,512]{1,0:T(8,128)(2,1)} %bitcast.6, s32[3,320]{1,0:T(4,128)} %bitcast.9, s32[1,64]{1,0:T(1,128)} %bitcast.11, bf16[100,320]{1,0:T(8,128)(2,1)} %target_hbm.1, bf16[512,512]{1,0:T(8,128)(2,1)} %ws_hbm.1, ...), custom_call_target="tpu_custom_call" | custom-call | tf_op jit(solution)/shard_map/decoder_crps_step/pallas_call | solution.py:560
  61.7 1.5 %unpack.1 = (f32[320]{0:T(512)}, f32[8,512]{1,0:T(8,128)}, f32[8,512]{1,0:T(8,128)}, f32[8,512]{1,0:T(8,128)}, f32[8,100]{1,0:T(8,128)}) custom-call(f32[2,8,384]{2,1,0:T(8,128)} %get-tuple-element.7.crow_ref, f32[2,4,16,128]{3,2,1,0:T(8,128)} %get-tuple-element.8.final_ref), custom_call_target="tpu_custom_call" | custom-call | tf_op jit(solution)/shard_map/unpack/pallas_call | solution.py:618

commit v4 on v3

--- a/solution.py
+++ b/solution.py
@@ -455,14 +455,42 @@
     away = (zl + y // 2) % 2
     owner = away == 0
 
-    def z_copy(j, g):
+    def z_copy(j, g, skip=0):
         k = 2 * j + away
-        n = pl.ds(SLOT_AT[g], SLOTS[g])
+        n = pl.ds(SLOT_AT[g] + skip, SLOTS[g] - skip)
         return rcopy(slab.at[((z + k) % 8) // 2, n], z_in.at[k, n], s_z.at[g, j], r_z.at[g, k], z_peer(k))
 
-    def z_arrived(k, g):
-        n = pl.ds(SLOT_AT[g], SLOTS[g])
+    def z_each(j, g, act):
+        if g > 0:
+            act(z_copy(j, g))
+            return
+        wanted = ((z + 2 * j + away) % 8) // 4 == y % 2
+
+        @pl.when(wanted)
+        def _():
+            act(z_copy(j, 0))
+
+        @pl.when(jnp.logical_not(wanted))
+        def _():
+            act(z_copy(j, 0, 1))
+
+    def z_start(j, g):
+        z_each(j, g, lambda cp: cp.start())
+
+    def z_sent(j, g):
+        z_each(j, g, lambda cp: cp.wait_send())
+
+    def z_arrived(k, g, skip=0):
+        n = pl.ds(SLOT_AT[g] + skip, SLOTS[g] - skip)
         rcopy(slab.at[0, n], z_in.at[k, n], s_z.at[g, 0], r_z.at[g, k], z_peer(8)).wait_recv()
+
+    def z_sum(g, skip=0):
+        n = pl.ds(SLOT_AT[g] + skip, SLOTS[g] - skip)
+        acc = slab[zl // 2, n].astype(F32)
+        for k in (1, 15, 2, 14, 3, 13, 4, 12, 5, 11, 6, 10, 7, 9, 8):
+            z_arrived(k, g, skip)
+            acc = acc + z_in[k, n].astype(F32)
+        final[y % 2, n] = acc
 
     def g_copy(k, g):
         n = pl.ds(SLOT_AT[g], SLOTS[g])
@@ -484,22 +512,30 @@
         for h in range(2):
             slab[2 + h, hi - 1] = done2[h]
         for j in (4, 3, 5, 2, 6, 1, 7):
-            z_copy(j, g).start()
+            z_start(j, g)
 
         @pl.when(away == 1)
         def _(g=g):
-            z_copy(0, g).start()
+            z_start(0, g)
 
 
     @pl.when(owner)
     def _():
         for g in range(3):
-            n = pl.ds(SLOT_AT[g], SLOTS[g])
-            acc = slab[zl // 2, n].astype(F32)
-            for k in (1, 15, 2, 14, 3, 13, 4, 12, 5, 11, 6, 10, 7, 9, 8):
-                z_arrived(k, g)
-                acc = acc + z_in[k, n].astype(F32)
-            final[y % 2, n] = acc
+            if g > 0:
+                z_sum(g)
+            else:
+                holds = zl // 4 == y % 2
+
+                @pl.when(holds)
+                def _():
+                    z_sum(0)
+
+                @pl.when(jnp.logical_not(holds))
+                def _():
+                    final[y % 2, 0] = jnp.zeros((16, 128), F32)
+                    z_sum(0, 1)
+
             for k in (2, 1, 3):
                 g_copy(k, g).start()
 
@@ -521,11 +557,11 @@
     @pl.when(away == 1)
     def _():
         for g in range(3):
-            z_copy(0, g).wait_send()
+            z_sent(0, g)
 
     for g in range(3):
         for j in range(1, 8):
-            z_copy(j, g).wait_send()
+            z_sent(j, g)
     for cp in direct:
         cp.wait_send()
 

time: 63.4 us -> 63.4 us (level)
  no operation moved by 1% of the time
where the time goes in v4:
time: 63.4 us; the launch traced here: 63.2 us
  Pallas kernels  62.6 us (99%)
  between operations  0.64 us (1%)
    pallas_call x1, Pallas kernels, per_device(): pl.pallas_call(kernel, out_shape=(shape((2, 8, 384), F32), shape((2, 4, 1...  61.1 us
    pallas_call x1, Pallas kernels, per_device(): pl.pallas_call(unpack, out_shape=(shape((PTS,), F32), shape((8, D), F32),...  1.49 us

profile of v4, /device:TPU:8, one launch (start us, length us, event | category | flops | bytes accessed | tf_op | source)
XLA Modules:
  0.0 63.2 jit_solution(7336960964361345888)
XLA Ops:
  0.6 61.1 %decoder_crps_step.1 = (f32[2,8,384]{2,1,0:T(8,128)}, f32[2,4,16,128]{3,2,1,0:T(8,128)}) custom-call(bf16[128,512]{1,0:T(8,128)(2,1)} %bitcast.7, bf16[320,512]{1,0:T(8,128)(2,1)} %bitcast.6, s32[3,320]{1,0:T(4,128)} %bitcast.9, s32[1,64]{1,0:T(1,128)} %bitcast.11, bf16[100,320]{1,0:T(8,128)(2,1)} %target_hbm.1, bf16[512,512]{1,0:T(8,128)(2,1)} %ws_hbm.1, ...), custom_call_target="tpu_custom_call" | custom-call | tf_op jit(solution)/shard_map/decoder_crps_step/pallas_call | solution.py:596
  61.7 1.5 %unpack.1 = (f32[320]{0:T(512)}, f32[8,512]{1,0:T(8,128)}, f32[8,512]{1,0:T(8,128)}, f32[8,512]{1,0:T(8,128)}, f32[8,100]{1,0:T(8,128)}) custom-call(f32[2,8,384]{2,1,0:T(8,128)} %get-tuple-element.7.crow_ref, f32[2,4,16,128]{3,2,1,0:T(8,128)} %get-tuple-element.8.final_ref), custom_call_target="tpu_custom_call" | custom-call | tf_op jit(solution)/shard_map/unpack/pallas_call | solution.py:654
